TPU v7x, 32 devices: a whole 2x2x4 slice. The times are simulated.
32 devices in a mesh: leaf: 4 (over y, x), row: 4 (over z), col: 2 (over core).
Axes of the slice: x: 2, y: 2, z: 4, core: 2. Of those that a mesh axis runs over, the one named last changes fastest.
Arguments:
- rhs_leaf: bfloat16 [4, 12288, 256], P('leaf', 'col'), may hold values from -6 to 6
- rhs_parent: bfloat16 [16384, 256], P(('leaf', 'row', 'col')), may hold values from -6 to 6
- inv_leaf: bfloat16 [4, 12288, 12288], P('leaf', 'row', 'col'), as said below
- panel: bfloat16 [4, 6144, 12288], P('leaf', 'col', 'row'), may hold values from -0.0546875 to 0.0546875
- row_map: int32 [4, 6144], P('leaf', 'col'), may hold values from 0 to 16383, as said below
- inv_parent: bfloat16 [16384, 16384], P(('row', 'col'), 'leaf'), as said below
Outputs:
- sol_leaf: bfloat16 [4, 12288, 256], P('leaf', 'col')
- sol_parent: bfloat16 [16384, 256], P(('leaf', 'row', 'col'))
Inputs may be any that keep to these rules, and one draw needn't show every extreme that they name: Within one leaf the 6144 entries of row_map are distinct parent rows. Split the parent rows into 32 owner blocks of 16384 // 32 consecutive rows: in each aligned block of 768 consecutive entries of a leaf, at most 24 entries fall in one owner block, and exactly 24 in some. `inv_leaf`: lower triangular: zeros above the diagonal, diagonal entries between 0.5 and 2. `inv_parent`: lower triangular: zeros above the diagonal, diagonal entries between 0.5 and 2.
All inputs are finite; a program needn't handle non-finite values.
Results may differ from a plain program's by a relative error of at most 0.01.
Values may be sent and summed in bfloat16 or wider, within the bound.
No kernel may reach another device: no remote copies, remote signals or barrier semaphores. Data moves between devices by JAX's collectives and lax.ppermute only.
A program may use at most 192 MiB of HBM per device.

v0:
```python
import jax
import jax.numpy as jnp
from jax import lax
from jax.sharding import PartitionSpec as P


def dense_updates(update, row_map, rhs_parent):
    total_rows = rhs_parent.shape[0] * lax.axis_size(("leaf", "row", "col"))
    dense = jnp.zeros((total_rows, rhs_parent.shape[1]), jnp.float32)
    dense = dense.at[row_map[0]].add(-update)
    offset = lax.axis_index(("leaf", "row", "col")) * rhs_parent.shape[0]
    own_rows = lax.dynamic_slice_in_dim(dense, offset, rhs_parent.shape[0], 0) + rhs_parent.astype(
        jnp.float32
    )
    return lax.dynamic_update_slice_in_dim(dense, own_rows, offset, 0)


def per_device(rhs_leaf, rhs_parent, inv_leaf, panel, row_map, inv_parent):
    leaf_part = jnp.dot(inv_leaf[0], rhs_leaf[0], preferred_element_type=jnp.float32)
    forward = lax.psum(leaf_part, "col").astype(jnp.bfloat16)
    update = jnp.dot(panel[0], forward, preferred_element_type=jnp.float32)
    dense = dense_updates(update, row_map, rhs_parent)
    leaf_block = lax.psum_scatter(dense, "leaf", scatter_dimension=0, tiled=True)
    reduced = lax.psum(leaf_block, ("row", "col")).astype(jnp.bfloat16)
    parent_part = jnp.dot(inv_parent, reduced, preferred_element_type=jnp.float32)
    fwd_parent = lax.psum(parent_part, "leaf").astype(jnp.bfloat16)
    back_part = lax.dot_general(
        inv_parent, fwd_parent, (((0,), (0,)), ((), ())), preferred_element_type=jnp.float32
    )
    sol_parent = lax.psum_scatter(
        back_part, ("row", "col"), scatter_dimension=0, tiled=True
    ).astype(jnp.bfloat16)
    whole_parent = lax.all_gather(sol_parent, ("leaf", "row", "col"), axis=0, tiled=True)
    picked = jnp.take(whole_parent, row_map[0], axis=0)
    coupling_part = lax.dot_general(
        panel[0], picked, (((0,), (0,)), ((), ())), preferred_element_type=jnp.float32
    )
    coupling = lax.psum(coupling_part, "col")
    corrected = (forward.astype(jnp.float32) - coupling).astype(jnp.bfloat16)
    final_part = lax.dot_general(
        inv_leaf[0], corrected, (((0,), (0,)), ((), ())), preferred_element_type=jnp.float32
    )
    sol_leaf = lax.psum(final_part, "row").astype(jnp.bfloat16)
    return (sol_leaf[None], sol_parent)


def solution(mesh):
    in_specs = (
        P("leaf", "col", None),
        P(("leaf", "row", "col"), None),
        P("leaf", "row", "col"),
        P("leaf", "col", "row"),
        P("leaf", "col"),
        P(("row", "col"), "leaf"),
    )
    out_specs = (P("leaf", "col", None), P(("leaf", "row", "col"), None))
    return jax.shard_map(
        per_device, mesh=mesh, in_specs=in_specs, out_specs=out_specs, check_vma=False
    )
```

profile of v0, /device:TPU:0, one launch (start us, length us, event | category | flops | bytes accessed | tf_op | source)
XLA Modules:
  0.0 867.6 jit_solution(15029139074675203361)
XLA Ops:
  7.2 0.0 copy-start
  7.2 0.0 reduce-scatter.3.cloned.1.call-start
  7.2 1.8 copy-done
  9.1 17.7 %fusion.2 = f32[3072,256]{1,0:T(8,128)} fusion(bf16[1,3072,6144]{2,1,0:T(8,128)(2,1)} %param.8, bf16[1,6144,256]{2,1,0:T(8,128)(2,1)S(1)} %copy-done), kind=kOutput, calls=%fused_computation.4 | convolution fusion | flops 9663676416 | bytes 44040192 | tf_op jit(solution)/shard_map/dot_general | solution.py:19
  26.8 12.6 %all-reduce.7 = bf16[3072,256]{1,0:T(8,128)(2,1)S(1)} all-reduce(f32[3072,256]{1,0:T(8,128)} %fusion.2), channel_id=1, replica_groups=mesh['leaf'=4,'row'=4,'col'=2] {'col'}, use_global_device_ids=true, to_apply=%region_0.0 | all-reduce | flops 786432 | bytes 4718592 | tf_op jit(solution)/shard_map/psum | solution.py:20
  39.4 11.0 %fusion.16 = f32[3072,256]{0,1:T(8,128)} fusion(bf16[1,3072,3072]{2,1,0:T(8,128)(2,1)} %param.9, bf16[3072,256]{1,0:T(8,128)(2,1)S(1)} %all-reduce.7), kind=kOutput, calls=%fused_computation.15 | convolution fusion | flops 4832624640 | bytes 23592960 | tf_op jit(solution)/shard_map/dot_general | solution.py:21
  50.4 0.0 copy-start.4
  50.4 3.6 copy.12
  53.9 0.0 copy-done.4
  53.9 0.0 copy-start.3
  53.9 24.1 %scatter_custom_fusion = f32[16384,256]{1,0:T(8,128)} fusion(s32[3072]{0:T(1024)S(1)} %bitcast.44, f32[3072,256]{1,0:T(8,128)} %copy.12, f32[]{:T(128)} %constant.14.clone.1), kind=kCustom, calls=%fused_computation.10 | custom fusion | flops 786432 | bytes 16777728 | tf_op jit(solution)/shard_map/scatter-add | solution.py:10
  78.1 0.0 copy-done.3
  78.1 1.9 add_dynamic-update-slice_fusion
  80.0 0.0 reduce-scatter.3.cloned.1.call-update
  80.0 0.0 reduce-scatter.5.cloned.1.call-start
  80.1 156.3 %reduce-scatter.3.cloned.1.call-done = f32[4096,256]{1,0:T(8,128)} async-done(((f32[16384,256]{1,0:T(8,128)}), f32[4096,256]{1,0:T(8,128)}) %reduce-scatter.3.cloned.1.call-update) | async-done | bytes 4194320 | tf_op jit(solution)/shard_map/reduce_scatter | solution.py:23
  236.4 89.0 %all-reduce.8 = bf16[4096,256]{1,0:T(8,128)(2,1)} all-reduce(f32[4096,256]{1,0:T(8,128)} %reduce-scatter.3.cloned.1.call-done), channel_id=1, replica_groups=mesh['leaf'=4,'row'=4,'col'=2] {'row','col'}, use_global_device_ids=true, to_apply=%region_3.0 | all-reduce | flops 1048576 | bytes 6291456 | tf_op jit(solution)/shard_map/psum | solution.py:24
  325.4 12.3 %convolution_bitcast_fusion.1 = f32[2048,256]{0,1:T(8,128)} fusion(bf16[2048,4096]{1,0:T(8,128)(2,1)} %param.11, bf16[4096,256]{1,0:T(8,128)(2,1)} %all-reduce.8), kind=kOutput, calls=%fused_computation.20 | convolution fusion | flops 4294967296 | bytes 20971520 | tf_op jit(solution)/shard_map/dot_general | solution.py:25
  337.7 71.1 %all-reduce.9 = bf16[2048,256]{0,1:T(8,128)(2,1)S(1)} all-reduce(f32[2048,256]{0,1:T(8,128)} %convolution_bitcast_fusion.1), channel_id=1, replica_groups=mesh['leaf'=4,'row'=4,'col'=2] {'leaf'}, use_global_device_ids=true, to_apply=%region_4.0 | all-reduce | flops 524288 | bytes 3145728 | tf_op jit(solution)/shard_map/psum | solution.py:26
  408.8 10.1 %convolution_bitcast_fusion = f32[4096,256]{0,1:T(8,128)} fusion(bf16[2048,4096]{1,0:T(8,128)(2,1)} %param.11, bf16[2048,256]{0,1:T(8,128)(2,1)S(1)} %all-reduce.9), kind=kOutput, calls=%fused_computation.13 | convolution fusion | flops 4294967296 | bytes 22020096 | tf_op jit(solution)/shard_map/dot_general | solution.py:27
  418.9 0.0 reduce-scatter.5.cloned.1.call-update
  418.9 0.0 all-gather.2.cloned.1.call-start
  419.0 53.0 %reduce-scatter.5.cloned.1.call-done = f32[512,256]{0,1:T(8,128)} async-done(((f32[4096,256]{0,1:T(8,128)}), f32[512,256]{0,1:T(8,128)}) %reduce-scatter.5.cloned.1.call-update) | async-done | bytes 524304 | tf_op jit(solution)/shard_map/reduce_scatter | solution.py:30
  472.0 1.8 convert_element_type.29
  473.8 0.0 all-gather.2.cloned.1.call-update
  473.8 0.3 all-reduce.6.cloned.1.call-start
  474.1 84.1 %all-gather.2.cloned.1.call-done = bf16[16384,256]{0,1:T(8,128)(2,1)} async-done(((bf16[512,256]{0,1:T(8,128)(2,1)}), bf16[16384,256]{0,1:T(8,128)(2,1)}) %all-gather.2.cloned.1.call-update) | async-done | bytes 8388624 | tf_op jit(solution)/shard_map/all_gather | solution.py:33
  558.2 11.9 %copy.13 = bf16[16384,256]{1,0:T(8,128)(2,1)} copy(bf16[16384,256]{0,1:T(8,128)(2,1)} %all-gather.2.cloned.1.call-done) | data formatting | bytes 16777216 | tf_op jit(solution)/shard_map/all_gather | solution.py:33
  570.1 14.3 %gather_fusion = bf16[3072,256]{1,0:T(8,128)(2,1)S(1)} fusion(bf16[16384,256]{1,0:T(8,128)(2,1)} %copy.13, s32[3072]{0:T(1024)S(1)} %broadcast_clamp_fusion), kind=kCustom, calls=%fused_computation | custom fusion | bytes 3158016 | tf_op jit(solution)/shard_map/jit(_take)/gather | solution.py:34
  584.3 12.7 %fusion.19 = f32[3072,256]{1,0:T(8,128)} fusion(bf16[1,3072,3072]{2,1,0:T(8,128)(2,1)} %param.9, bf16[3072,256]{1,0:T(8,128)(2,1)S(1)} %gather_fusion, pred[3072]{0:T(1024)(128)(4,1)S(1)} %compare_and_fusion), kind=kOutput, calls=%fused_computation.16 | convolution fusion | flops 4832624640 | bytes 23596032 | tf_op jit(solution)/shard_map/dot_general | solution.py:35
  597.0 0.0 copy-start.2
  597.0 0.0 all-reduce.6.cloned.1.call-update
  597.0 0.9 copy-done.2
  597.9 0.8 copy.15
  598.8 19.8 %all-reduce.6.cloned.1.call-done = f32[3072,256]{1,0:T(8,128)} async-done(((f32[3072,256]{1,0:T(8,128)}), f32[3072,256]{1,0:T(8,128)}) %all-reduce.6.cloned.1.call-update) | async-done | bytes 3145744 | tf_op jit(solution)/shard_map/psum | solution.py:38
  618.6 19.5 %fusion.10 = f32[6144,256]{0,1:T(8,128)} fusion(bf16[1,3072,6144]{2,1,0:T(8,128)(2,1)} %param.8, f32[3072,256]{1,0:T(8,128)} %all-reduce.6.cloned.1.call-done, bf16[3072,256]{1,0:T(8,128)(2,1)S(1)} %all-reduce.7), kind=kOutput, calls=%fused_computation.12 | convolution fusion | flops 9666035712 | bytes 48758784 | tf_op jit(solution)/shard_map/dot_general | solution.py:40
  638.1 218.2 %all-reduce.10 = bf16[6144,256]{0,1:T(8,128)(2,1)} all-reduce(f32[6144,256]{0,1:T(8,128)} %fusion.10), channel_id=1, replica_groups=mesh['leaf'=4,'row'=4,'col'=2] {'row'}, use_global_device_ids=true, to_apply=%region_7.8 | all-reduce | flops 1572864 | bytes 9437184 | tf_op jit(solution)/shard_map/psum | solution.py:43
  856.3 0.0 copy-start.1
  856.3 4.8 copy.14
  861.1 0.0 copy-done.1
  (3 shorter events, 0.0 us)
Async XLA Ops:
  7.2 1.9 copy-start
  7.2 229.2 %reduce-scatter.3.cloned.1.call-start = ((), (), s32[]{:S(2)}) async-start(), calls=%async_computation.2 | async-start | bytes 20971520 | tf_op jit(solution)/shard_map/reduce_scatter | solution.py:23
  50.4 3.6 copy-start.4
  53.9 24.2 %copy-start.3 = (bf16[512,256]{1,0:T(8,128)(2,1)S(1)}, bf16[512,256]{1,0:T(8,128)(2,1)}, u32[]{:S(2)}) copy-start(bf16[512,256]{1,0:T(8,128)(2,1)} %param.7) | copy-start | bytes 786436
  80.0 392.0 %reduce-scatter.5.cloned.1.call-start = ((), (), s32[]{:S(2)}) async-start(), calls=%async_computation.3 | async-start | bytes 4718592 | tf_op jit(solution)/shard_map/reduce_scatter | solution.py:30
  418.9 139.3 %all-gather.2.cloned.1.call-start = ((), (), s32[]{:S(2)}) async-start(), calls=%async_computation.4 | async-start | bytes 8650752 | tf_op jit(solution)/shard_map/all_gather | solution.py:33
  473.8 144.8 %all-reduce.6.cloned.1.call-start = ((), (), s32[]{:S(2)}) async-start(), calls=%async_computation.5 | async-start | bytes 6291456 | tf_op jit(solution)/shard_map/psum | solution.py:38
  597.0 0.9 copy-start.2
  856.3 4.8 copy-start.1
Sparse Core Ops, SparseCore 0:
  80.1 156.2 reduce-scatter.2
  419.0 52.9 reduce-scatter.4
  475.5 82.6 all-gather.1
  597.1 21.3 all-reduce.5
where the time goes:
time: 868 us
  blocking collectives  391 us (45%)
  waiting for transfers between devices  313 us (36%)
  matrix products  83.3 us (10%)
  local copies, waits for them, and re-layouts  38.1 us (4%)
  other arithmetic  27.8 us (3%)
  between operations  13.8 us (2%)
    psum x1, blocking collectives, per_device(): sol_leaf = lax.psum(final_part, 'row').astype(jnp.bfloat16)  218 us
    reduce_scatter x1, waiting for transfers between devices, per_device(): lax.psum_scatter(dense, 'leaf', scatter_dimension=0, tiled=True)  156 us
    psum x1, blocking collectives, per_device(): reduced = lax.psum(leaf_block, ('row', 'col')).astype(jnp.bfloat16)  89 us
    all_gather x1, waiting for transfers between devices, per_device(): lax.all_gather(sol_parent, ('leaf', 'row', 'col'), axis=0, tiled=True)  84.1 us
    psum x1, blocking collectives, per_device(): fwd_parent = lax.psum(parent_part, 'leaf').astype(jnp.bfloat16)  71.1 us
    reduce_scatter x1, waiting for transfers between devices, per_device(): lax.psum_scatter(back_part, ('row', 'col'), scatter_dimension=0, tiled=True)  53 us
    scatter-add x1, other arithmetic, dense_updates(): dense = dense.at[row_map[0]].add(-update)  24.1 us
    psum x1, waiting for transfers between devices, per_device(): coupling = lax.psum(coupling_part, 'col')  19.8 us
  transfers between devices with their start and end apart: 4, of which 4 were waited for; matrix products, arithmetic and copies ran while one was open for 0% of the time, Pallas kernels for 0%

commit v1 on v0

v1 whole, which is shorter than its diff:
```python
import jax
import jax.numpy as jnp
from jax import lax
from jax.sharding import PartitionSpec as P

ALL = ("leaf", "row", "col")
F32 = jnp.float32
BF16 = jnp.bfloat16
CHUNKS = 8


def matmul(a, x):
    return jnp.dot(a, x, preferred_element_type=F32)


def matmul_t(a, x):
    return lax.dot_general(a, x, (((0,), (0,)), ((), ())), preferred_element_type=F32)


def sum_cores(part):
    if lax.axis_size("col") == 2:
        other = lax.ppermute(part.astype(BF16), "col", [(0, 1), (1, 0)])
        return part + other.astype(F32)
    return lax.psum(part, "col")


def sum_leaves(part):
    size = lax.axis_size("leaf")
    bits = [1 << b for b in range(size.bit_length() - 1)]
    halves = jnp.split(part, 2, axis=0)
    orders = (bits, bits[::-1])
    for step in range(len(bits)):
        moved = [
            lax.ppermute(h.astype(BF16), "leaf", [(i, i ^ order[step]) for i in range(size)])
            for h, order in zip(halves, orders)
        ]
        halves = [h + m.astype(F32) for h, m in zip(halves, moved)]
    return jnp.concatenate(halves, axis=0).astype(BF16)


def gather_block(own):
    rows, cols = own.shape
    depth = lax.axis_size("row")
    z = lax.axis_index("row")
    parts = [own]
    for d in range(1, depth):
        parts.append(lax.ppermute(own, "row", [(i, (i + d) % depth) for i in range(depth)]))
    stacked = jnp.stack(parts)
    placed = jnp.take(stacked, (z - jnp.arange(depth)) % depth, axis=0, mode="clip")
    cores = lax.axis_size("col")
    if cores == 2:
        c = lax.axis_index("col")
        other = lax.ppermute(placed, "col", [(0, 1), (1, 0)])
        both = jnp.stack(
            [jnp.where(c == 0, placed, other), jnp.where(c == 0, other, placed)], axis=1
        )
    else:
        both = lax.all_gather(placed, "col", axis=1)
    return both.reshape(depth * cores * rows, cols)


def scatter_block(part):
    depth = lax.axis_size("row")
    cores = lax.axis_size("col")
    z = lax.axis_index("row")
    rows = part.shape[0] // (depth * cores)
    split = part.reshape(depth, cores, rows, part.shape[1])
    if cores == 2:
        c = lax.axis_index("col")
        mine = lax.dynamic_index_in_dim(split, c, 1, keepdims=False)
        theirs = lax.dynamic_index_in_dim(split, 1 - c, 1, keepdims=False).astype(BF16)
        summed = mine + lax.ppermute(theirs, "col", [(0, 1), (1, 0)]).astype(F32)
    else:
        summed = lax.psum_scatter(split, "col", scatter_dimension=1, tiled=True)[:, 0]
    total = lax.dynamic_index_in_dim(summed, z, 0, keepdims=False)
    summed = summed.astype(BF16)
    for d in range(1, depth):
        chunk = lax.dynamic_index_in_dim(summed, (z + d) % depth, 0, keepdims=False)
        moved = lax.ppermute(chunk, "row", [(i, (i + d) % depth) for i in range(depth)])
        total = total + moved.astype(F32)
    return total.astype(BF16)


def sum_rows(part):
    depth = lax.axis_size("row")
    z = lax.axis_index("row")
    size = part.shape[0] // CHUNKS
    down = [(i + 1, i) for i in range(depth - 1)]
    up = [(i, i + 1) for i in range(depth - 1)]

    def chunk(array, j):
        return lax.dynamic_slice_in_dim(array, jnp.clip(j, 0, CHUNKS - 1) * size, size, 0)

    def add(array, j, moved):
        old = chunk(array, j)
        new = jnp.where((j >= 0) & (j < CHUNKS), old + moved, old)
        return lax.dynamic_update_slice_in_dim(array, new, jnp.clip(j, 0, CHUNKS - 1) * size, 0)

    total = part
    from_above = jnp.zeros((size, part.shape[1]), BF16)
    from_below = from_above
    for step in range(CHUNKS + depth - 2):
        send_down = chunk(part, step - (depth - 1) + z) + from_above
        send_up = chunk(part, step - z) + from_below
        from_above = lax.ppermute(send_down, "row", down)
        from_below = lax.ppermute(send_up, "row", up)
        total = add(total, step - depth + 2 + z, from_above)
        total = add(total, step - z + 1, from_below)
    return total


def slots_of(row_map, own, devices, depth):
    blocks = row_map.reshape(depth, -1)
    size = blocks.shape[1]
    cap = -(-size // devices)
    owner = blocks // own
    earlier = jnp.arange(size)[None, :] < jnp.arange(size)[:, None]
    rank = jnp.sum((owner[:, :, None] == owner[:, None, :]) & earlier[None], axis=2, dtype=jnp.int32)
    slot = owner * cap + rank
    hit = slot[:, None, :] == jnp.arange(devices * cap, dtype=jnp.int32)[None, :, None]
    local = jnp.max(jnp.where(hit, (blocks % own)[:, None, :], -1), axis=2)
    local = local.reshape(depth, devices, cap).transpose(1, 0, 2).reshape(devices, depth * cap)
    return hit.astype(BF16), local


def per_device(rhs_leaf, rhs_parent, inv_leaf, panel, row_map, inv_parent):
    leaves, depth, cores = (lax.axis_size(a) for a in ALL)
    devices = leaves * depth * cores
    me = lax.axis_index(ALL)
    own, width = rhs_parent.shape

    pick, local = slots_of(row_map[0], own, devices, depth)
    per_owner = local.shape[1]
    cap = per_owner // depth
    lists = lax.all_gather(local, ("leaf", "col"))
    mine = lax.dynamic_index_in_dim(lists, me, 1, keepdims=False).reshape(-1)
    place = (mine[None, :] == jnp.arange(own, dtype=jnp.int32)[:, None]).astype(BF16)

    forward = sum_cores(matmul(inv_leaf[0], rhs_leaf[0])).astype(BF16)
    update = matmul(panel[0], forward).astype(BF16).reshape(depth, -1, width)
    packed = jnp.einsum("bsi,bir->bsr", pick, update, preferred_element_type=F32).astype(BF16)
    packed = packed.reshape(depth, devices, cap, width).transpose(1, 0, 2, 3)
    packed = packed.reshape(devices * per_owner, width)
    arrived = lax.all_to_all(packed, ALL, 0, 0, tiled=True)
    arrived = arrived.reshape(leaves, depth, cores * per_owner, width).astype(F32).sum(1)
    arrived = arrived.reshape(leaves * cores * per_owner, width).astype(BF16)
    reduced = (rhs_parent.astype(F32) - matmul(place, arrived)).astype(BF16)

    fwd_parent = sum_leaves(matmul(inv_parent, gather_block(reduced)))
    sol_parent = scatter_block(matmul_t(inv_parent, fwd_parent))

    wanted = matmul_t(place, sol_parent).astype(BF16)
    wanted = wanted.reshape(leaves, 1, cores * per_owner, width)
    wanted = jnp.broadcast_to(wanted, (leaves, depth, cores * per_owner, width))
    got = lax.all_to_all(wanted.reshape(devices * per_owner, width), ALL, 0, 0, tiled=True)
    got = got.reshape(devices, depth, cap, width).transpose(1, 0, 2, 3)
    got = got.reshape(depth, devices * cap, width)
    picked = jnp.einsum("bsi,bsr->bir", pick, got, preferred_element_type=F32).astype(BF16)
    picked = picked.reshape(panel.shape[1], width)

    coupling = sum_cores(matmul_t(panel[0], picked))
    corrected = (forward.astype(F32) - coupling).astype(BF16)
    sol_leaf = sum_rows(matmul_t(inv_leaf[0], corrected).astype(BF16))
    return (sol_leaf[None], sol_parent)


def solution(mesh):
    in_specs = (
        P("leaf", "col", None),
        P(("leaf", "row", "col"), None),
        P("leaf", "row", "col"),
        P("leaf", "col", "row"),
        P("leaf", "col"),
        P(("row", "col"), "leaf"),
    )
    out_specs = (P("leaf", "col", None), P(("leaf", "row", "col"), None))
    return jax.shard_map(
        per_device, mesh=mesh, in_specs=in_specs, out_specs=out_specs, check_vma=False
    )
```

time: 868 us -> 481 us (0.55)
  blocking collectives: 391 us -> 61.6 us
  waiting for transfers between devices: 313 us -> 127 us
  starting transfers between devices: 0.39 us -> 96.6 us
  other arithmetic: 27.8 us -> 56.1 us
  between operations: 13.8 us -> 1.54 us
    psum x4 -> x0, blocking collectives: 391 us -> none  [the longest x1 218 us: per_device(): sol_leaf = lax.psum(final_part, 'row').astype(jnp.bfloat16)]
    reduce_scatter x2 -> x0, waiting for transfers between devices: 209 us -> none  [the longest x1 156 us: per_device(): lax.psum_scatter(dense, 'leaf', scatter_dimension=0, tiled=True)]
    ppermute x0 -> x34, waiting for transfers between devices: none -> 103 us  [the longest x10 28.3 us: sum_rows(): from_above = lax.ppermute(send_down, 'row', down)]
    ppermute x0 -> x34, starting transfers between devices: none -> 89.6 us  [the longest x10 51.6 us: sum_rows(): from_below = lax.ppermute(send_up, 'row', up)]
    all_gather x1 -> x0, waiting for transfers between devices: 84.1 us -> none  [per_device(): lax.all_gather(sol_parent, ('leaf', 'row', 'col'), axis=0, tiled=True)]
    all_to_all x0 -> x1, blocking collectives: none -> 48.2 us  [per_device(): lax.all_to_all(wanted.reshape(devices * per_owner, width), ALL, 0, 0, til...]
    scatter-add x1 -> x0, other arithmetic: 24.1 us -> none  [dense_updates(): dense = dense.at[row_map[0]].add(-update)]
    all_to_all x0 -> x1, waiting for transfers between devices: none -> 23.4 us  [per_device(): arrived = lax.all_to_all(packed, ALL, 0, 0, tiled=True)]
  transfers between devices with their start and end apart: 4 -> 35, of which waited for: 4 -> 30; matrix products, arithmetic and copies ran while one was open for 0% -> 9% of each run, Pallas kernels for 0% -> 0%
where the time goes in v1:
time: 481 us; the launch traced here: 475 us
  waiting for transfers between devices  127 us (26%)
  starting transfers between devices  96.6 us (20%)
  matrix products  88.4 us (18%)
  blocking collectives  61.6 us (13%)
  other arithmetic  56.1 us (12%)
  local copies, waits for them, and re-layouts  43.7 us (9%)
    ppermute x10, starting transfers between devices, sum_rows(): from_below = lax.ppermute(send_up, 'row', up)  51.6 us
    all_to_all x1, blocking collectives, per_device(): lax.all_to_all(wanted.reshape(devices * per_owner, width), ALL, 0, 0, til...  48.2 us
    dot_general x4, matrix products, matmul_t(): lax.dot_general(a, x, (((0,), (0,)), ((), ())), preferred_element_type=F32)  44.1 us
    dot_general x4, matrix products, matmul(): return jnp.dot(a, x, preferred_element_type=F32)  39.1 us
    ppermute x10, waiting for transfers between devices, sum_rows(): from_above = lax.ppermute(send_down, 'row', down)  28.3 us
    ppermute x4, waiting for transfers between devices, sum_leaves(): lax.ppermute(h.astype(BF16), 'leaf', [(i, i ^ order[step]) for i in range...  24.1 us
    dynamic_update_slice x12, other arithmetic, add(): lax.dynamic_update_slice_in_dim(array, new, jnp.clip(j, 0, CHUNKS - 1) *...  23.7 us
    all_to_all x1, waiting for transfers between devices, per_device(): arrived = lax.all_to_all(packed, ALL, 0, 0, tiled=True)  23.4 us
  transfers between devices with their start and end apart: 35, of which 30 were waited for; matrix products, arithmetic and copies ran while one was open for 9% of the time, Pallas kernels for 0%

profile of v1, /device:TPU:0, one launch (start us, length us, event | category | flops | bytes accessed | tf_op | source)
XLA Modules:
  0.0 474.7 jit_solution(5019758265459458606)
XLA Ops:
  2.5 18.4 %fusion.70 = (bf16[3072,256]{1,0:T(8,128)(2,1)}, f32[3072,256]{1,0:T(8,128)}) fusion(bf16[1,6144,256]{2,1,0:T(8,128)(2,1)S(1)} %copy-done, bf16[1,3072,6144]{2,1,0:T(8,128)(2,1)} %param.8), kind=kOutput, calls=%fused_computation.143 | convolution fusion | flops 9664462848 | bytes 45613056 | tf_op jit(solution)/shard_map/dot_general | solution.py:13
  25.1 11.4 %fusion.21 = bf16[3072,256]{0,1:T(8,128)(2,1)} fusion(bf16[1,3072,3072]{2,1,0:T(8,128)(2,1)} %param.9, f32[3072,256]{1,0:T(8,128)} %get-tuple-element.55, bf16[3072,256]{1,0:T(8,128)(2,1)S(1)} %collective-permute-done), kind=kOutput, calls=%fused_computation.20 | convolution fusion | flops 4834983936 | bytes 25165824 | tf_op jit(solution)/shard_map/dot_general | solution.py:13
  38.2 3.4 fusion.25
  43.0 7.0 %all-to-all-start = ((bf16[32,96,256]{2,1,0:T(8,128)(2,1)}), bf16[32,96,256]{2,1,0:T(8,128)(2,1)S(1)}, u32[]{:S(2)}, u32[]{:S(2)}) async-start(bf16[32,96,256]{2,1,0:T(8,128)(2,1)} %bitcast.8), calls=%async_computation | async-start | bytes 3145728 | tf_op jit(solution)/shard_map/all_to_all | solution.py:144
  51.9 13.4 %all_gather.3 = s32[8,32,96]{2,1,0:T(8,128)S(1)} all-gather(s32[1,32,96]{2,1,0:T(8,128)S(1)} %all_gather_reshape.3), channel_id=1, replica_groups=mesh['leaf'=4,'row'=4,'col'=2] {'leaf','col'}, dimensions={0}, use_global_device_ids=true | all-gather | bytes 110592 | tf_op jit(solution)/shard_map/all_gather | solution.py:135
  65.4 23.4 %all-to-all-done = bf16[32,96,256]{2,1,0:T(8,128)(2,1)S(1)} async-done(((bf16[32,96,256]{2,1,0:T(8,128)(2,1)}), bf16[32,96,256]{2,1,0:T(8,128)(2,1)S(1)}, u32[]{:S(2)}, u32[]{:S(2)}) %all-to-all-start) | async-done | bytes 1572896 | tf_op jit(solution)/shard_map/all_to_all | solution.py:144
  90.1 3.5 collective-permute-start.3
  93.5 7.3 %collective-permute-done.1 = bf16[512,256]{1,0:T(8,128)(2,1)S(1)} collective-permute-done((bf16[512,256]{1,0:T(8,128)(2,1)S(1)}, bf16[512,256]{1,0:T(8,128)(2,1)S(1)}, u32[]{:S(2)}, u32[]{:S(2)}) %collective-permute-start.1) | collective-permute-done | bytes 262176 | tf_op jit(solution)/shard_map/ppermute | solution.py:47
  100.8 10.0 %collective-permute-done.2 = bf16[512,256]{1,0:T(8,128)(2,1)S(1)} collective-permute-done((bf16[512,256]{1,0:T(8,128)(2,1)S(1)}, bf16[512,256]{1,0:T(8,128)(2,1)S(1)}, u32[]{:S(2)}, u32[]{:S(2)}) %collective-permute-start.2) | collective-permute-done | bytes 262176 | tf_op jit(solution)/shard_map/ppermute | solution.py:47
  111.6 2.6 collective-permute-done.4
  116.1 8.8 %convolution_bitcast_fusion.1 = f32[2048,256]{0,1:T(8,128)S(1)} fusion(bf16[4096,256]{1,0:T(8,128)(2,1)} %bitcast.145, bf16[2048,4096]{1,0:T(8,128)(2,1)} %param.11), kind=kOutput, calls=%fused_computation.24 | convolution fusion | flops 4294967296 | bytes 20971520 | tf_op jit(solution)/shard_map/dot_general | solution.py:13
  126.5 12.6 %collective-permute-done.5 = bf16[1024,256]{0,1:T(8,128)(2,1)S(1)} collective-permute-done((bf16[1024,256]{0,1:T(8,128)(2,1)S(1)}, bf16[1024,256]{0,1:T(8,128)(2,1)S(1)}, u32[]{:S(2)}, u32[]{:S(2)}) %collective-permute-start.5) | collective-permute-done | bytes 524320 | tf_op jit(solution)/shard_map/ppermute | solution.py:34
  143.0 10.9 %collective-permute-done.6 = bf16[1024,256]{0,1:T(8,128)(2,1)} collective-permute-done((bf16[1024,256]{0,1:T(8,128)(2,1)}, bf16[1024,256]{0,1:T(8,128)(2,1)}, u32[]{:S(2)}, u32[]{:S(2)}) %collective-permute-start.6) | collective-permute-done | bytes 524320 | tf_op jit(solution)/shard_map/ppermute | solution.py:34
  156.1 10.3 %convolution_bitcast_fusion = f32[4096,256]{0,1:T(8,128)} fusion(bf16[2048,4096]{1,0:T(8,128)(2,1)} %param.11, bf16[1024,256]{0,1:T(8,128)(2,1)S(1)} %get-tuple-element.34, bf16[1024,256]{0,1:T(8,128)(2,1)S(1)} %get-tuple-element.33), kind=kOutput, calls=%fused_computation.15 | convolution fusion | flops 4297064448 | bytes 22020096 | tf_op jit(solution)/shard_map/dot_general | solution.py:17
  166.4 6.6 %reshape.196 = f32[4,2,512,256]{2,1,0,3:T(2,128)} reshape(f32[4096,256]{0,1:T(8,128)} %convolution_bitcast_fusion) | data formatting | bytes 8388608 | tf_op jit(solution)/shard_map/reshape | solution.py:67
  173.0 4.3 constant_dynamic-slice_fusion
  179.3 5.7 %constant_dynamic-slice_fusion.1 = f32[4,1,512,256]{2,1,0,3:T(1,128)} fusion(f32[4,2,512,256]{2,1,0,3:T(2,128)} %reshape.196, s32[]{:T(128)S(6)} %select_n.329), kind=kLoop, calls=%fused_computation.127 | loop fusion | bytes 4194308 | tf_op jit(solution)/shard_map/jit(dynamic_index_in_dim)/dynamic_slice | solution.py:70
  185.0 4.6 copy.41
  189.6 2.9 fusion.68
  192.5 14.3 %collective-permute-start.10 = (bf16[512,256]{1,0:T(8,128)(2,1)S(1)}, bf16[512,256]{1,0:T(8,128)(2,1)S(1)}, u32[]{:S(2)}, u32[]{:S(2)}) collective-permute-start(bf16[512,256]{1,0:T(8,128)(2,1)S(1)} %get-tuple-element.41), channel_id=1, source_target_pairs={{0,2},{2,4},{4,6},{6,0},{1,3},{3,5},{5,7},{7,1},{8,10},{10,12},{12... | collective-permute-start | bytes 786440 | tf_op jit(solution)/shard_map/ppermute | solution.py:79
  209.2 4.7 collective-permute-done.10
  213.9 11.0 %collective-permute-done.11 = bf16[512,256]{1,0:T(8,128)(2,1)S(1)} collective-permute-done((bf16[512,256]{1,0:T(8,128)(2,1)S(1)}, bf16[512,256]{1,0:T(8,128)(2,1)S(1)}, u32[]{:S(2)}, u32[]{:S(2)}) %collective-permute-start.11) | collective-permute-done | bytes 262176 | tf_op jit(solution)/shard_map/ppermute | solution.py:79
  226.8 48.2 %all_to_all.18 = bf16[32,96,256]{2,1,0:T(8,128)(2,1)S(1)} all-to-all(bf16[32,96,256]{2,1,0:T(8,128)(2,1)S(1)} %bitcast.144), channel_id=1, replica_groups=mesh['leaf'=4,'row'=4,'col'=2] {'leaf','row','col'}, dimensions={0} | all-to-all | bytes 3145728 | tf_op jit(solution)/shard_map/all_to_all | solution.py:155
  277.0 13.1 %fusion.71 = (bf16[3072,256]{1,0:T(8,128)(2,1)S(1)}, f32[3072,256]{1,0:T(8,128)}) fusion(bf16[3072,256]{1,0:T(8,128)(2,1)S(1)} %bitcast.157, bf16[1,3072,3072]{2,1,0:T(8,128)(2,1)} %param.9), kind=kOutput, calls=%fused_computation.144 | convolution fusion | flops 4832624640 | bytes 25165824 | tf_op jit(solution)/shard_map/dot_general | solution.py:17
  290.1 3.4 collective-permute-done.13
  294.6 20.1 %fusion.10 = bf16[256,6144]{1,0:T(8,128)(2,1)S(1)} fusion(bf16[1,3072,6144]{2,1,0:T(8,128)(2,1)} %param.8, f32[3072,256]{1,0:T(8,128)} %get-tuple-element.57, bf16[3072,256]{1,0:T(8,128)(2,1)} %copy-done.3, f32[3072,256]{1,0:T(8,128)} %get-tuple-element.55, bf16[3072,256]{1,0:T(8,128)(2,1)} %copy-done.2), kind=kOutput, calls=%fused_computation.14 | convolution fusion | flops 9671540736 | bytes 50331648 | tf_op jit(solution)/shard_map/dot_general | solution.py:17
  317.1 4.6 collective-permute-start.15
  323.3 5.8 %collective-permute-done.14 = bf16[768,256]{0,1:T(8,128)(2,1)} collective-permute-done((bf16[768,256]{0,1:T(8,128)(2,1)}, bf16[768,256]{0,1:T(8,128)(2,1)}, u32[]{:S(2)}, u32[]{:S(2)}) %collective-permute-start.14) | collective-permute-done | bytes 393248 | tf_op jit(solution)/shard_map/ppermute | solution.py:105
  333.9 5.1 %collective-permute-start.17 = (bf16[768,256]{0,1:T(8,128)(2,1)}, bf16[768,256]{0,1:T(8,128)(2,1)S(1)}, u32[]{:S(2)}, u32[]{:S(2)}) collective-permute-start(bf16[768,256]{0,1:T(8,128)(2,1)} %get-tuple-element.30), channel_id=1, source_target_pairs={{0,2},{2,4},{4,6},{1,3},{3,5},{5,7},{8,10},{10,12},{12,14},{9,11},... | collective-permute-start | bytes 1179656 | tf_op jit(solution)/shard_map/ppermute | solution.py:106
  341.0 4.4 collective-permute-done.16
  346.6 2.4 bitcast_add_fusion.16
  350.3 5.6 %collective-permute-start.19 = (bf16[768,256]{0,1:T(8,128)(2,1)}, bf16[768,256]{0,1:T(8,128)(2,1)}, u32[]{:S(2)}, u32[]{:S(2)}) collective-permute-start(bf16[768,256]{0,1:T(8,128)(2,1)} %get-tuple-element.28), channel_id=1, source_target_pairs={{0,2},{2,4},{4,6},{1,3},{3,5},{5,7},{8,10},{10,12},{12,14},{9,11},... | collective-permute-start | bytes 1179656 | tf_op jit(solution)/shard_map/ppermute | solution.py:106
  357.8 3.2 collective-permute-done.18
  362.2 2.5 bitcast_add_fusion.14
  366.0 5.1 %collective-permute-start.21 = (bf16[768,256]{0,1:T(8,128)(2,1)}, bf16[768,256]{0,1:T(8,128)(2,1)S(1)}, u32[]{:S(2)}, u32[]{:S(2)}) collective-permute-start(bf16[768,256]{0,1:T(8,128)(2,1)} %get-tuple-element.26), channel_id=1, source_target_pairs={{0,2},{2,4},{4,6},{1,3},{3,5},{5,7},{8,10},{10,12},{12,14},{9,11},... | collective-permute-start | bytes 1179656 | tf_op jit(solution)/shard_map/ppermute | solution.py:106
  373.0 2.9 collective-permute-done.20
  380.7 5.7 %collective-permute-start.23 = (bf16[768,256]{0,1:T(8,128)(2,1)}, bf16[768,256]{0,1:T(8,128)(2,1)}, u32[]{:S(2)}, u32[]{:S(2)}) collective-permute-start(bf16[768,256]{0,1:T(8,128)(2,1)} %get-tuple-element.24), channel_id=1, source_target_pairs={{0,2},{2,4},{4,6},{1,3},{3,5},{5,7},{8,10},{10,12},{12,14},{9,11},... | collective-permute-start | bytes 1179656 | tf_op jit(solution)/shard_map/ppermute | solution.py:106
  391.3 2.5 bitcast_add_fusion.10
  395.1 5.0 %collective-permute-start.25 = (bf16[768,256]{0,1:T(8,128)(2,1)}, bf16[768,256]{0,1:T(8,128)(2,1)S(1)}, u32[]{:S(2)}, u32[]{:S(2)}) collective-permute-start(bf16[768,256]{0,1:T(8,128)(2,1)} %get-tuple-element.22), channel_id=1, source_target_pairs={{0,2},{2,4},{4,6},{1,3},{3,5},{5,7},{8,10},{10,12},{12,14},{9,11},... | collective-permute-start | bytes 1179656 | tf_op jit(solution)/shard_map/ppermute | solution.py:106
  405.7 2.5 bitcast_add_fusion.8
  409.5 4.9 %collective-permute-start.27 = (bf16[768,256]{0,1:T(8,128)(2,1)}, bf16[768,256]{0,1:T(8,128)(2,1)S(1)}, u32[]{:S(2)}, u32[]{:S(2)}) collective-permute-start(bf16[768,256]{0,1:T(8,128)(2,1)} %get-tuple-element.20), channel_id=1, source_target_pairs={{0,2},{2,4},{4,6},{1,3},{3,5},{5,7},{8,10},{10,12},{12,14},{9,11},... | collective-permute-start | bytes 1179656 | tf_op jit(solution)/shard_map/ppermute | solution.py:106
  420.0 2.5 bitcast_add_fusion.6
  423.8 5.0 %collective-permute-start.29 = (bf16[768,256]{0,1:T(8,128)(2,1)}, bf16[768,256]{0,1:T(8,128)(2,1)S(1)}, u32[]{:S(2)}, u32[]{:S(2)}) collective-permute-start(bf16[768,256]{0,1:T(8,128)(2,1)} %get-tuple-element.18), channel_id=1, source_target_pairs={{0,2},{2,4},{4,6},{1,3},{3,5},{5,7},{8,10},{10,12},{12,14},{9,11},... | collective-permute-start | bytes 1179656 | tf_op jit(solution)/shard_map/ppermute | solution.py:106
  434.4 2.5 bitcast_add_fusion.4
  438.2 5.3 %collective-permute-start.31 = (bf16[768,256]{0,1:T(8,128)(2,1)}, bf16[768,256]{0,1:T(8,128)(2,1)S(1)}, u32[]{:S(2)}, u32[]{:S(2)}) collective-permute-start(bf16[768,256]{0,1:T(8,128)(2,1)} %get-tuple-element.16), channel_id=1, source_target_pairs={{0,2},{2,4},{4,6},{1,3},{3,5},{5,7},{8,10},{10,12},{12,14},{9,11},... | collective-permute-start | bytes 1179656 | tf_op jit(solution)/shard_map/ppermute | solution.py:106
  452.7 5.3 %collective-permute-start.33 = (bf16[768,256]{0,1:T(8,128)(2,1)}, bf16[768,256]{0,1:T(8,128)(2,1)S(1)}, u32[]{:S(2)}, u32[]{:S(2)}) collective-permute-start(bf16[768,256]{0,1:T(8,128)(2,1)} %get-tuple-element.14), channel_id=1, source_target_pairs={{0,2},{2,4},{4,6},{1,3},{3,5},{5,7},{8,10},{10,12},{12,14},{9,11},... | collective-permute-start | bytes 1179656 | tf_op jit(solution)/shard_map/ppermute | solution.py:106
  463.9 3.8 copy.69
  469.8 4.6 copy.45
  (116 shorter events, 100.2 us)
Async XLA Ops:
  0.6 1.9 copy-start
  0.6 21.3 %copy-start.9 = (s32[1,3072]{1,0:T(1,128)S(1)}, s32[1,3072]{1,0:T(1,128)}, u32[]{:S(2)}) copy-start(s32[1,3072]{1,0:T(1,128)} %param.10) | copy-start | bytes 36868
  21.0 4.1 collective-permute-start
  25.1 11.5 %copy-start.2 = (bf16[3072,256]{1,0:T(8,128)(2,1)}, bf16[3072,256]{1,0:T(8,128)(2,1)S(1)}, u32[]{:S(2)}) copy-start(bf16[3072,256]{1,0:T(8,128)(2,1)S(1)} %collective-permute-done) | copy-start | bytes 4718596
  43.0 46.2 %copy-start.10 = (bf16[512,256]{1,0:T(8,128)(2,1)S(1)}, bf16[512,256]{1,0:T(8,128)(2,1)}, u32[]{:S(2)}) copy-start(bf16[512,256]{1,0:T(8,128)(2,1)} %param.7) | copy-start | bytes 786436
  43.0 45.8 %all-to-all-start = ((bf16[32,96,256]{2,1,0:T(8,128)(2,1)}), bf16[32,96,256]{2,1,0:T(8,128)(2,1)S(1)}, u32[]{:S(2)}, u32[]{:S(2)}) async-start(bf16[32,96,256]{2,1,0:T(8,128)(2,1)} %bitcast.8), calls=%async_computation | async-start | bytes 3145728 | tf_op jit(solution)/shard_map/all_to_all | solution.py:144
  89.6 11.2 %collective-permute-start.1 = (bf16[512,256]{1,0:T(8,128)(2,1)S(1)}, bf16[512,256]{1,0:T(8,128)(2,1)S(1)}, u32[]{:S(2)}, u32[]{:S(2)}) collective-permute-start(bf16[512,256]{1,0:T(8,128)(2,1)S(1)} %fusion.31), channel_id=1, source_target_pairs={{0,2},{2,4},{4,6},{6,0},{1,3},{3,5},{5,7},{7,1},{8,10},{10,12},{12... | collective-permute-start | bytes 786440 | tf_op jit(solution)/shard_map/ppermute | solution.py:47
  89.7 21.1 %collective-permute-start.2 = (bf16[512,256]{1,0:T(8,128)(2,1)S(1)}, bf16[512,256]{1,0:T(8,128)(2,1)S(1)}, u32[]{:S(2)}, u32[]{:S(2)}) collective-permute-start(bf16[512,256]{1,0:T(8,128)(2,1)S(1)} %fusion.31), channel_id=1, source_target_pairs={{0,4},{2,6},{4,0},{6,2},{1,5},{3,7},{5,1},{7,3},{8,12},{10,14},{12... | collective-permute-start | bytes 786440 | tf_op jit(solution)/shard_map/ppermute | solution.py:47
  90.1 20.7 %collective-permute-start.3 = (bf16[512,256]{1,0:T(8,128)(2,1)S(1)}, bf16[512,256]{1,0:T(8,128)(2,1)S(1)}, u32[]{:S(2)}, u32[]{:S(2)}) collective-permute-start(bf16[512,256]{1,0:T(8,128)(2,1)S(1)} %fusion.31), channel_id=1, source_target_pairs={{0,6},{2,0},{4,2},{6,4},{1,7},{3,1},{5,3},{7,5},{8,14},{10,8},{12,... | collective-permute-start | bytes 786440 | tf_op jit(solution)/shard_map/ppermute | solution.py:47
  111.5 2.7 collective-permute-start.4
  125.0 14.0 %collective-permute-start.5 = (bf16[1024,256]{0,1:T(8,128)(2,1)S(1)}, bf16[1024,256]{0,1:T(8,128)(2,1)S(1)}, u32[]{:S(2)}, u32[]{:S(2)}) collective-permute-start(bf16[1024,256]{0,1:T(8,128)(2,1)S(1)} %get-tuple-element.37), channel_id=1, source_target_pairs={{0,8},{8,0},{16,24},{24,16},{1,9},{9,1},{17,25},{25,17},{2,10},{10... | collective-permute-start | bytes 1572872 | tf_op jit(solution)/shard_map/ppermute | solution.py:34
  125.4 13.7 %collective-permute-start.7 = (bf16[1024,256]{0,1:T(8,128)(2,1)S(1)}, bf16[1024,256]{0,1:T(8,128)(2,1)S(1)}, u32[]{:S(2)}, u32[]{:S(2)}) collective-permute-start(bf16[1024,256]{0,1:T(8,128)(2,1)S(1)} %get-tuple-element.38), channel_id=1, source_target_pairs={{0,16},{8,24},{16,0},{24,8},{1,17},{9,25},{17,1},{25,9},{2,18},{10... | collective-permute-start | bytes 1572872 | tf_op jit(solution)/shard_map/ppermute | solution.py:34
  140.5 13.4 %collective-permute-start.6 = (bf16[1024,256]{0,1:T(8,128)(2,1)}, bf16[1024,256]{0,1:T(8,128)(2,1)}, u32[]{:S(2)}, u32[]{:S(2)}) collective-permute-start(bf16[1024,256]{0,1:T(8,128)(2,1)} %get-tuple-element.35), channel_id=1, source_target_pairs={{0,16},{8,24},{16,0},{24,8},{1,17},{9,25},{17,1},{25,9},{2,18},{10... | collective-permute-start | bytes 1572872 | tf_op jit(solution)/shard_map/ppermute | solution.py:34
  141.5 12.9 %collective-permute-start.8 = (bf16[1024,256]{0,1:T(8,128)(2,1)}, bf16[1024,256]{0,1:T(8,128)(2,1)}, u32[]{:S(2)}, u32[]{:S(2)}) collective-permute-start(bf16[1024,256]{0,1:T(8,128)(2,1)} %get-tuple-element.36), channel_id=1, source_target_pairs={{0,8},{8,0},{16,24},{24,16},{1,9},{9,1},{17,25},{25,17},{2,10},{10... | collective-permute-start | bytes 1572872 | tf_op jit(solution)/shard_map/ppermute | solution.py:34
  179.1 10.4 %collective-permute-start.9 = (bf16[4,512,256]{2,1,0:T(8,128)(2,1)S(1)}, bf16[4,512,256]{2,1,0:T(8,128)(2,1)}, u32[]{:S(2)}, u32[]{:S(2)}) collective-permute-start(bf16[4,512,256]{2,1,0:T(8,128)(2,1)S(1)} %bitcast.149), channel_id=1, source_target_pairs={{0,1},{1,0},{2,3},{3,2},{4,5},{5,4},{6,7},{7,6},{8,9},{9,8},{10,11... | collective-permute-start | bytes 3145736 | tf_op jit(solution)/shard_map/ppermute | solution.py:72
  192.5 21.4 %collective-permute-start.10 = (bf16[512,256]{1,0:T(8,128)(2,1)S(1)}, bf16[512,256]{1,0:T(8,128)(2,1)S(1)}, u32[]{:S(2)}, u32[]{:S(2)}) collective-permute-start(bf16[512,256]{1,0:T(8,128)(2,1)S(1)} %get-tuple-element.41), channel_id=1, source_target_pairs={{0,2},{2,4},{4,6},{6,0},{1,3},{3,5},{5,7},{7,1},{8,10},{10,12},{12... | collective-permute-start | bytes 786440 | tf_op jit(solution)/shard_map/ppermute | solution.py:79
  206.8 18.1 %collective-permute-start.11 = (bf16[512,256]{1,0:T(8,128)(2,1)S(1)}, bf16[512,256]{1,0:T(8,128)(2,1)S(1)}, u32[]{:S(2)}, u32[]{:S(2)}) collective-permute-start(bf16[512,256]{1,0:T(8,128)(2,1)S(1)} %get-tuple-element.43), channel_id=1, source_target_pairs={{0,4},{2,6},{4,0},{6,2},{1,5},{3,7},{5,1},{7,3},{8,12},{10,14},{12... | collective-permute-start | bytes 786440 | tf_op jit(solution)/shard_map/ppermute | solution.py:79
  207.2 17.7 %collective-permute-start.12 = (bf16[512,256]{1,0:T(8,128)(2,1)S(1)}, bf16[512,256]{1,0:T(8,128)(2,1)S(1)}, u32[]{:S(2)}, u32[]{:S(2)}) collective-permute-start(bf16[512,256]{1,0:T(8,128)(2,1)S(1)} %get-tuple-element.42), channel_id=1, source_target_pairs={{0,6},{2,0},{4,2},{6,4},{1,7},{3,1},{5,3},{7,5},{8,14},{10,8},{12,... | collective-permute-start | bytes 786440 | tf_op jit(solution)/shard_map/ppermute | solution.py:79
  226.0 0.8 copy-start.8
  290.1 3.4 collective-permute-start.13
  293.5 1.2 copy-start.3
  315.8 13.3 %collective-permute-start.14 = (bf16[768,256]{0,1:T(8,128)(2,1)}, bf16[768,256]{0,1:T(8,128)(2,1)}, u32[]{:S(2)}, u32[]{:S(2)}) collective-permute-start(bf16[768,256]{0,1:T(8,128)(2,1)} %get-tuple-element.32), channel_id=1, source_target_pairs={{2,0},{4,2},{6,4},{3,1},{5,3},{7,5},{10,8},{12,10},{14,12},{11,9},... | collective-permute-start | bytes 1179656 | tf_op jit(solution)/shard_map/ppermute | solution.py:105
  317.1 13.2 %collective-permute-start.15 = (bf16[768,256]{0,1:T(8,128)(2,1)}, bf16[768,256]{0,1:T(8,128)(2,1)S(1)}, u32[]{:S(2)}, u32[]{:S(2)}) collective-permute-start(bf16[768,256]{0,1:T(8,128)(2,1)} %get-tuple-element.31), channel_id=1, source_target_pairs={{0,2},{2,4},{4,6},{1,3},{3,5},{5,7},{8,10},{10,12},{12,14},{9,11},... | collective-permute-start | bytes 1179656 | tf_op jit(solution)/shard_map/ppermute | solution.py:106
  330.3 3.6 copy-start.7
  332.6 12.8 %collective-permute-start.16 = (bf16[768,256]{0,1:T(8,128)(2,1)}, bf16[768,256]{0,1:T(8,128)(2,1)}, u32[]{:S(2)}, u32[]{:S(2)}) collective-permute-start(bf16[768,256]{0,1:T(8,128)(2,1)} %get-tuple-element.11), channel_id=1, source_target_pairs={{2,0},{4,2},{6,4},{3,1},{5,3},{7,5},{10,8},{12,10},{14,12},{11,9},... | collective-permute-start | bytes 1179656 | tf_op jit(solution)/shard_map/ppermute | solution.py:105
  333.9 12.7 %collective-permute-start.17 = (bf16[768,256]{0,1:T(8,128)(2,1)}, bf16[768,256]{0,1:T(8,128)(2,1)S(1)}, u32[]{:S(2)}, u32[]{:S(2)}) collective-permute-start(bf16[768,256]{0,1:T(8,128)(2,1)} %get-tuple-element.30), channel_id=1, source_target_pairs={{0,2},{2,4},{4,6},{1,3},{3,5},{5,7},{8,10},{10,12},{12,14},{9,11},... | collective-permute-start | bytes 1179656 | tf_op jit(solution)/shard_map/ppermute | solution.py:106
  349.0 12.0 %collective-permute-start.18 = (bf16[768,256]{0,1:T(8,128)(2,1)}, bf16[768,256]{0,1:T(8,128)(2,1)}, u32[]{:S(2)}, u32[]{:S(2)}) collective-permute-start(bf16[768,256]{0,1:T(8,128)(2,1)} %get-tuple-element.29), channel_id=1, source_target_pairs={{2,0},{4,2},{6,4},{3,1},{5,3},{7,5},{10,8},{12,10},{14,12},{11,9},... | collective-permute-start | bytes 1179656 | tf_op jit(solution)/shard_map/ppermute | solution.py:105
  350.3 11.9 %collective-permute-start.19 = (bf16[768,256]{0,1:T(8,128)(2,1)}, bf16[768,256]{0,1:T(8,128)(2,1)}, u32[]{:S(2)}, u32[]{:S(2)}) collective-permute-start(bf16[768,256]{0,1:T(8,128)(2,1)} %get-tuple-element.28), channel_id=1, source_target_pairs={{0,2},{2,4},{4,6},{1,3},{3,5},{5,7},{8,10},{10,12},{12,14},{9,11},... | collective-permute-start | bytes 1179656 | tf_op jit(solution)/shard_map/ppermute | solution.py:106
  364.7 11.2 %collective-permute-start.20 = (bf16[768,256]{0,1:T(8,128)(2,1)}, bf16[768,256]{0,1:T(8,128)(2,1)}, u32[]{:S(2)}, u32[]{:S(2)}) collective-permute-start(bf16[768,256]{0,1:T(8,128)(2,1)} %get-tuple-element.27), channel_id=1, source_target_pairs={{2,0},{4,2},{6,4},{3,1},{5,3},{7,5},{10,8},{12,10},{14,12},{11,9},... | collective-permute-start | bytes 1179656 | tf_op jit(solution)/shard_map/ppermute | solution.py:105
  366.0 11.1 %collective-permute-start.21 = (bf16[768,256]{0,1:T(8,128)(2,1)}, bf16[768,256]{0,1:T(8,128)(2,1)S(1)}, u32[]{:S(2)}, u32[]{:S(2)}) collective-permute-start(bf16[768,256]{0,1:T(8,128)(2,1)} %get-tuple-element.26), channel_id=1, source_target_pairs={{0,2},{2,4},{4,6},{1,3},{3,5},{5,7},{8,10},{10,12},{12,14},{9,11},... | collective-permute-start | bytes 1179656 | tf_op jit(solution)/shard_map/ppermute | solution.py:106
  379.5 10.4 %collective-permute-start.22 = (bf16[768,256]{0,1:T(8,128)(2,1)}, bf16[768,256]{0,1:T(8,128)(2,1)}, u32[]{:S(2)}, u32[]{:S(2)}) collective-permute-start(bf16[768,256]{0,1:T(8,128)(2,1)} %get-tuple-element.25), channel_id=1, source_target_pairs={{2,0},{4,2},{6,4},{3,1},{5,3},{7,5},{10,8},{12,10},{14,12},{11,9},... | collective-permute-start | bytes 1179656 | tf_op jit(solution)/shard_map/ppermute | solution.py:105
  380.7 10.5 %collective-permute-start.23 = (bf16[768,256]{0,1:T(8,128)(2,1)}, bf16[768,256]{0,1:T(8,128)(2,1)}, u32[]{:S(2)}, u32[]{:S(2)}) collective-permute-start(bf16[768,256]{0,1:T(8,128)(2,1)} %get-tuple-element.24), channel_id=1, source_target_pairs={{0,2},{2,4},{4,6},{1,3},{3,5},{5,7},{8,10},{10,12},{12,14},{9,11},... | collective-permute-start | bytes 1179656 | tf_op jit(solution)/shard_map/ppermute | solution.py:106
  393.8 10.4 %collective-permute-start.24 = (bf16[768,256]{0,1:T(8,128)(2,1)}, bf16[768,256]{0,1:T(8,128)(2,1)}, u32[]{:S(2)}, u32[]{:S(2)}) collective-permute-start(bf16[768,256]{0,1:T(8,128)(2,1)} %get-tuple-element.23), channel_id=1, source_target_pairs={{2,0},{4,2},{6,4},{3,1},{5,3},{7,5},{10,8},{12,10},{14,12},{11,9},... | collective-permute-start | bytes 1179656 | tf_op jit(solution)/shard_map/ppermute | solution.py:105
  395.1 10.6 %collective-permute-start.25 = (bf16[768,256]{0,1:T(8,128)(2,1)}, bf16[768,256]{0,1:T(8,128)(2,1)S(1)}, u32[]{:S(2)}, u32[]{:S(2)}) collective-permute-start(bf16[768,256]{0,1:T(8,128)(2,1)} %get-tuple-element.22), channel_id=1, source_target_pairs={{0,2},{2,4},{4,6},{1,3},{3,5},{5,7},{8,10},{10,12},{12,14},{9,11},... | collective-permute-start | bytes 1179656 | tf_op jit(solution)/shard_map/ppermute | solution.py:106
  405.7 3.8 copy-start.6
  408.2 10.3 %collective-permute-start.26 = (bf16[768,256]{0,1:T(8,128)(2,1)}, bf16[768,256]{0,1:T(8,128)(2,1)}, u32[]{:S(2)}, u32[]{:S(2)}) collective-permute-start(bf16[768,256]{0,1:T(8,128)(2,1)} %get-tuple-element.21), channel_id=1, source_target_pairs={{2,0},{4,2},{6,4},{3,1},{5,3},{7,5},{10,8},{12,10},{14,12},{11,9},... | collective-permute-start | bytes 1179656 | tf_op jit(solution)/shard_map/ppermute | solution.py:105
  409.5 10.5 %collective-permute-start.27 = (bf16[768,256]{0,1:T(8,128)(2,1)}, bf16[768,256]{0,1:T(8,128)(2,1)S(1)}, u32[]{:S(2)}, u32[]{:S(2)}) collective-permute-start(bf16[768,256]{0,1:T(8,128)(2,1)} %get-tuple-element.20), channel_id=1, source_target_pairs={{0,2},{2,4},{4,6},{1,3},{3,5},{5,7},{8,10},{10,12},{12,14},{9,11},... | collective-permute-start | bytes 1179656 | tf_op jit(solution)/shard_map/ppermute | solution.py:106
  420.0 3.8 copy-start.5
  422.5 10.4 %collective-permute-start.28 = (bf16[768,256]{0,1:T(8,128)(2,1)}, bf16[768,256]{0,1:T(8,128)(2,1)}, u32[]{:S(2)}, u32[]{:S(2)}) collective-permute-start(bf16[768,256]{0,1:T(8,128)(2,1)} %get-tuple-element.19), channel_id=1, source_target_pairs={{2,0},{4,2},{6,4},{3,1},{5,3},{7,5},{10,8},{12,10},{14,12},{11,9},... | collective-permute-start | bytes 1179656 | tf_op jit(solution)/shard_map/ppermute | solution.py:105
  423.8 10.6 %collective-permute-start.29 = (bf16[768,256]{0,1:T(8,128)(2,1)}, bf16[768,256]{0,1:T(8,128)(2,1)S(1)}, u32[]{:S(2)}, u32[]{:S(2)}) collective-permute-start(bf16[768,256]{0,1:T(8,128)(2,1)} %get-tuple-element.18), channel_id=1, source_target_pairs={{0,2},{2,4},{4,6},{1,3},{3,5},{5,7},{8,10},{10,12},{12,14},{9,11},... | collective-permute-start | bytes 1179656 | tf_op jit(solution)/shard_map/ppermute | solution.py:106
  434.4 3.8 copy-start.4
  436.9 10.7 %collective-permute-start.30 = (bf16[768,256]{0,1:T(8,128)(2,1)}, bf16[768,256]{0,1:T(8,128)(2,1)}, u32[]{:S(2)}, u32[]{:S(2)}) collective-permute-start(bf16[768,256]{0,1:T(8,128)(2,1)} %get-tuple-element.17), channel_id=1, source_target_pairs={{2,0},{4,2},{6,4},{3,1},{5,3},{7,5},{10,8},{12,10},{14,12},{11,9},... | collective-permute-start | bytes 1179656 | tf_op jit(solution)/shard_map/ppermute | solution.py:105
  438.2 10.9 %collective-permute-start.31 = (bf16[768,256]{0,1:T(8,128)(2,1)}, bf16[768,256]{0,1:T(8,128)(2,1)S(1)}, u32[]{:S(2)}, u32[]{:S(2)}) collective-permute-start(bf16[768,256]{0,1:T(8,128)(2,1)} %get-tuple-element.16), channel_id=1, source_target_pairs={{0,2},{2,4},{4,6},{1,3},{3,5},{5,7},{8,10},{10,12},{12,14},{9,11},... | collective-permute-start | bytes 1179656 | tf_op jit(solution)/shard_map/ppermute | solution.py:106
  451.4 10.6 %collective-permute-start.32 = (bf16[768,256]{0,1:T(8,128)(2,1)}, bf16[768,256]{0,1:T(8,128)(2,1)S(1)}, u32[]{:S(2)}, u32[]{:S(2)}) collective-permute-start(bf16[768,256]{0,1:T(8,128)(2,1)} %get-tuple-element.15), channel_id=1, source_target_pairs={{2,0},{4,2},{6,4},{3,1},{5,3},{7,5},{10,8},{12,10},{14,12},{11,9},... | collective-permute-start | bytes 1179656 | tf_op jit(solution)/shard_map/ppermute | solution.py:105
  452.7 15.0 %collective-permute-start.33 = (bf16[768,256]{0,1:T(8,128)(2,1)}, bf16[768,256]{0,1:T(8,128)(2,1)S(1)}, u32[]{:S(2)}, u32[]{:S(2)}) collective-permute-start(bf16[768,256]{0,1:T(8,128)(2,1)} %get-tuple-element.14), channel_id=1, source_target_pairs={{0,2},{2,4},{4,6},{1,3},{3,5},{5,7},{8,10},{10,12},{12,14},{9,11},... | collective-permute-start | bytes 1179656 | tf_op jit(solution)/shard_map/ppermute | solution.py:106
  467.7 6.7 %copy-start.1 = (bf16[1,6144,256]{2,1,0:T(8,128)(2,1)S(1)}, bf16[1,6144,256]{2,1,0:T(8,128)(2,1)}, u32[]{:S(2)}) copy-start(bf16[1,6144,256]{2,1,0:T(8,128)(2,1)} %param.6) | copy-start | bytes 9437188
